TPU v7x, 256 devices: a whole 4x4x8 slice. The times are simulated.
256 devices in a mesh: fsdp: 8 (over x, core), ep: 32 (over z, y).
Axes of the slice: x: 4, y: 4, z: 8, core: 2. Of those that a mesh axis runs over, the one named last changes fastest.
Arguments:
- out_grad: bfloat16 [4096, 7168], P('ep', 'fsdp'), may hold values from -1.5 to 1.5
- router_input: bfloat16 [4096, 7168], P('ep', 'fsdp'), may hold values from -6 to 6
- router_weight: float32 [7168, 32], P('fsdp'), may hold values from -0.0625 to 0.0625
- routes: int32 [4096, 8], P('ep'), may hold values from 0 to 31, all different within a row; in each aligned block of 128 rows (0 to 127, 128 to 255, ...) at most 36 rows name the same one
- balance_grad: float32 [4096, 32], P('ep'), may hold values from -6 to 6
- saved_hidden: bfloat16 [32, 32, 36, 2048], P('ep', None, None, 'fsdp'), may hold values from -6 to 6
- expert_down: bfloat16 [32, 2048, 7168], P('ep', None, 'fsdp'), may hold values from -0.125 to 0.125
- attention_grads: bfloat16 [32, 4, 288, 7168], P('ep', None, None, 'fsdp'), may hold values from -6 to 6
Outputs:
- grad_hidden: bfloat16 [32, 32, 36, 2048], P('ep', None, None, 'fsdp')
- grad_down: bfloat16 [32, 2048, 7168], P('ep', None, 'fsdp')
- router_grad: float32 [7168, 32], P('fsdp')
- token_grad: bfloat16 [4096, 7168], P('ep', 'fsdp')
- muon_update: bfloat16 [4, 288, 7168], P(None, None, 'fsdp')
Inputs may be any that keep to these rules, and one draw needn't show every extreme that they name: `routes`: each expert is named by at most 36 of the rows of one device's block of 128 tokens, and by exactly 36 in some block; a row names 8 different experts.
All inputs are finite; a program needn't handle non-finite values.
Results may differ from a plain program's by a relative error of at most 0.029.
Values may be sent and summed in bfloat16 or wider, within the bound.
No kernel may reach another device: no remote copies, remote signals or barrier semaphores. Data moves between devices by JAX's collectives and lax.ppermute only.
A program may use at most 128 MiB of HBM per device.

v0:
```python
import jax
import jax.numpy as jnp
from jax import lax
from jax.sharding import PartitionSpec as P

D = 7168
LATENT = 288
NS_ITERS = 2


ROUTE_SCALE = 2.827
NORM_EPS = 1e-07
COEF_A = 3.4445
COEF_B = -4.775
COEF_C = 2.0315


def slot_tables(routes_block, experts, capacity):
    expert_ids = jnp.arange(experts, dtype=jnp.int32)
    chosen = jnp.any(routes_block[:, :, None] == expert_ids[None, None, :], axis=1)
    counted = jnp.cumsum(chosen.astype(jnp.int32), axis=0) - 1
    position = jnp.where(chosen, counted, -1)
    slot_ids = jnp.arange(capacity, dtype=jnp.int32)
    matches = position.T[:, None, :] == slot_ids[None, :, None]
    token_ids = jnp.arange(routes_block.shape[0], dtype=jnp.int32)
    source = jnp.sum(jnp.where(matches, token_ids[None, None, :], 0), axis=2)
    filled = jnp.any(matches, axis=2)
    return (chosen, matches, source, filled)


def local_gram(current):
    return jnp.einsum("mrd,msd->mrs", current, current, preferred_element_type=jnp.float32)


def orthogonalize(initial, gram_maker):
    current = initial
    for turn_index in range(NS_ITERS):
        gram_matrix = gram_maker(current).astype(jnp.bfloat16)
        square = jnp.einsum(
            "mrs,mst->mrt", gram_matrix, gram_matrix, preferred_element_type=jnp.float32
        )
        blended = (COEF_B * gram_matrix.astype(jnp.float32) + COEF_C * square).astype(jnp.bfloat16)
        product = jnp.einsum("mrs,msd->mrd", blended, current, preferred_element_type=jnp.float32)
        current = (COEF_A * current.astype(jnp.float32) + product).astype(jnp.bfloat16)
    factor = 0.2 * jnp.sqrt(jnp.float32(max(LATENT, D)))
    return (factor * current.astype(jnp.float32)).astype(jnp.bfloat16)


def merge_copies(returned, copies):
    grouped = returned.reshape(-1, copies, returned.shape[1], returned.shape[2]).astype(jnp.float32)
    return (jnp.sum(grouped, axis=1) * (1.0 / copies)).astype(jnp.bfloat16)


def on_device(
    out_grad,
    router_input,
    router_weight,
    routes,
    balance_grad,
    saved_hidden,
    expert_down,
    attention_grads,
):
    experts = router_weight.shape[1]
    capacity = saved_hidden.shape[2]
    partial_logits = jnp.dot(
        router_input.astype(jnp.float32), router_weight, precision=lax.Precision.HIGHEST
    )
    logits = lax.psum(partial_logits, "fsdp")
    scores = jax.nn.sigmoid(logits)
    chosen, matches, source, filled = slot_tables(routes, experts, capacity)
    selected = chosen.astype(jnp.float32)
    score_total = jnp.sum(selected * scores, axis=1, keepdims=True)
    gate_values = (selected * ROUTE_SCALE * scores / score_total).astype(jnp.bfloat16)
    gate_table = gate_values.T.astype(jnp.float32)[:, None, :]
    slot_gates = jnp.sum(jnp.where(matches, gate_table, 0.0), axis=2).astype(jnp.bfloat16)
    empty_value = jnp.zeros((), jnp.bfloat16)
    packed = jnp.where(filled[:, :, None], jnp.take(out_grad, source, axis=0), empty_value)
    slot_part, slot_gate = (
        lax.all_to_all(packed, "ep", split_axis=0, concat_axis=0, tiled=True),
        lax.all_to_all(slot_gates, "ep", split_axis=0, concat_axis=0, tiled=True),
    )
    rows_flat = slot_part.reshape(-1, slot_part.shape[2])
    gate_flat = slot_gate.reshape(-1, 1).astype(jnp.float32)
    down_local = expert_down[0]
    upstream_rows = lax.psum_scatter(
        lax.dot_general(
            down_local, rows_flat, (((1,), (1,)), ((), ())), preferred_element_type=jnp.float32
        ).astype(jnp.bfloat16),
        "fsdp",
        scatter_dimension=0,
        tiled=True,
    ).astype(jnp.float32)
    upstream = upstream_rows.T
    hidden_share = saved_hidden[0].reshape(-1, saved_hidden.shape[3])
    grad_hidden = (gate_flat * upstream).astype(jnp.bfloat16).reshape(saved_hidden.shape)
    gate_part = jnp.sum(hidden_share.astype(jnp.float32) * upstream, axis=1).reshape(
        slot_gate.shape
    )
    hidden_whole = lax.all_gather(saved_hidden, "fsdp", axis=3, tiled=True)
    hidden_flat = hidden_whole[0].reshape(-1, hidden_whole.shape[3])
    scaled = (gate_flat * rows_flat.astype(jnp.float32)).astype(jnp.bfloat16)
    grad_down = lax.dot_general(
        hidden_flat, scaled, (((0,), (0,)), ((), ())), preferred_element_type=jnp.float32
    )
    grad_down = grad_down.astype(jnp.bfloat16)[None]
    gate_grad = lax.psum(gate_part, "fsdp")
    returned = lax.all_to_all(gate_grad, "ep", split_axis=0, concat_axis=0, tiled=True)
    gate_back = jnp.sum(jnp.where(matches, returned[:, :, None], 0.0), axis=1).T
    weighted = jnp.sum(selected * gate_back * scores, axis=1, keepdims=True) / score_total
    score_grad = balance_grad + selected * (ROUTE_SCALE / score_total) * (gate_back - weighted)
    logit_grad = score_grad * scores * (1.0 - scores)
    router_part = jnp.dot(
        router_input.astype(jnp.float32).T, logit_grad, precision=lax.Precision.HIGHEST
    )
    router_grad = lax.psum(router_part.astype(jnp.bfloat16), "ep").astype(jnp.float32)
    token_grad = jnp.dot(logit_grad, router_weight.T, precision=lax.Precision.HIGHEST).astype(
        jnp.bfloat16
    )
    partial_value = attention_grads[0]
    copies = lax.axis_size("fsdp") // partial_value.shape[0]
    summed = lax.psum(partial_value.astype(jnp.float32).astype(jnp.bfloat16), "ep").astype(
        jnp.float32
    )
    squares = lax.psum(jnp.sum(summed * summed, axis=(1, 2)), "fsdp")
    initial = (summed / (jnp.sqrt(squares)[:, None, None] + NORM_EPS)).astype(jnp.bfloat16)
    owned_rows = lax.all_to_all(
        jnp.repeat(initial, copies, axis=0), "fsdp", split_axis=0, concat_axis=2, tiled=True
    )
    finished = orthogonalize(owned_rows, local_gram)
    muon_update = merge_copies(
        lax.all_to_all(finished, "fsdp", split_axis=2, concat_axis=0, tiled=True), copies
    )
    return (grad_hidden, grad_down, router_grad, token_grad, muon_update)


def solution(mesh):
    in_specs = (
        P("ep", "fsdp"),
        P("ep", "fsdp"),
        P("fsdp", None),
        P("ep", None),
        P("ep", None),
        P("ep", None, None, "fsdp"),
        P("ep", None, "fsdp"),
        P("ep", None, None, "fsdp"),
    )
    out_specs = (
        P("ep", None, None, "fsdp"),
        P("ep", None, "fsdp"),
        P("fsdp", None),
        P("ep", "fsdp"),
        P(None, None, "fsdp"),
    )
    return jax.shard_map(
        on_device, mesh=mesh, in_specs=in_specs, out_specs=out_specs, check_vma=False
    )
```

profile of v0, /device:TPU:2, one launch (start us, length us, event | category | flops | bytes accessed | tf_op | source)
XLA Modules:
  0.0 767.5 jit_solution(1338571680879707085)
XLA Ops:
  8.0 0.7 fusion.34
  8.8 0.1 copy.84
  9.0 0.2 reduce_window_sum.11
  9.2 0.7 select_reduce_fusion.1
  10.0 0.7 fusion.25
  10.8 0.1 reshape.170
  10.9 4.7 gather_fusion
  15.7 2.0 reshape.169
  17.9 2.9 select_select_fusion
  20.8 11.5 %all-to-all-start.1 = ((bf16[32,36,896]{2,1,0:T(8,128)(2,1)}), bf16[32,36,896]{2,1,0:T(8,128)(2,1)S(1)}, u32[]{:S(2)}, u32[]{:S(2)}) async-start(bf16[32,36,896]{2,1,0:T(8,128)(2,1)} %select_select_fusion), calls=%async_computation.1 | async-start | bytes 4587520 | tf_op jit(solution)/shard_map/all_to_all | solution.py:80
  32.3 0.7 all-reduce.3.cloned.1.call-update
  33.1 66.4 %all-to-all-done.1 = bf16[32,36,896]{2,1,0:T(8,128)(2,1)S(1)} async-done(((bf16[32,36,896]{2,1,0:T(8,128)(2,1)}), bf16[32,36,896]{2,1,0:T(8,128)(2,1)S(1)}, u32[]{:S(2)}, u32[]{:S(2)}) %all-to-all-start.1) | async-done | bytes 2064416 | tf_op jit(solution)/shard_map/all_to_all | solution.py:80
  99.5 1.9 reshape.157
  101.5 8.9 %fusion.6 = bf16[2048,1152]{0,1:T(8,128)(2,1)} fusion(bf16[1152,896]{1,0:T(8,128)(2,1)} %reshape.157, bf16[1,2048,896]{2,1,0:T(8,128)(2,1)} %param.14), kind=kOutput, calls=%fused_computation.11 | convolution fusion | flops 4230217728 | bytes 10452992 | tf_op jit(solution)/shard_map/dot_general | solution.py:87
  110.5 0.5 all-gather.2.cloned.1.call-update
  111.0 0.3 copy-done.4
  111.4 0.3 fusion.45
  111.7 1.4 copy.92
  113.1 2.4 reshape.165
  115.5 96.3 %all-reduce.3.cloned.1.call-done = bf16[4,288,896]{2,1,0:T(8,128)(2,1)} async-done(((bf16[4,288,896]{2,1,0:T(8,128)(2,1)}), bf16[4,288,896]{2,1,0:T(8,128)(2,1)}) %all-reduce.3.cloned.1.call-update) | async-done | bytes 2064400 | tf_op jit(solution)/shard_map/psum | solution.py:122
  211.8 2.2 fusion.7
  214.0 1.7 fusion.23
  215.7 0.1 all_to_all.35
  215.8 20.9 %all-reduce = (f32[32,1,36]{2,1,0:T(1,128)}, f32[128,32]{0,1:T(8,128)S(1)}, f32[4]{0:T(128)S(1)}) all-reduce(f32[32,1,36]{2,1,0:T(1,128)S(1)} %all_to_all.35, f32[128,32]{0,1:T(8,128)S(1)} %fusion.45, f32[4]{0:T(128)S(1)} %fusion.7), channel_id=1, replica_groups=mesh['fsdp'=8,'ep'=32] {'fsdp'}, use_global_device_ids=true, to_apply=%region_9.10 | all-reduce | flops 5252 | bytes 42016 | tf_op jit(solution)/shard_map/psum | solution.py:107
  236.7 5.8 all-to-all-start.2
  242.6 3.4 fusion.8
  246.0 6.2 all-to-all-done.2
  252.2 3.8 broadcast_in_dim.88
  256.1 8.1 %all-to-all-start.3 = ((bf16[8,288,896]{2,1,0:T(8,128)(2,1)}), bf16[8,288,896]{2,1,0:T(8,128)(2,1)}, u32[]{:S(2)}, u32[]{:S(2)}) async-start(bf16[8,288,896]{2,1,0:T(8,128)(2,1)} %bitcast.99), calls=%async_computation.4 | async-start | bytes 8257536 | tf_op jit(solution)/shard_map/all_to_all | solution.py:127
  264.2 0.2 select_reduce_fusion
  264.5 0.2 select_reduce_fusion.2
  264.9 0.6 copy.87
  265.5 46.3 %all-to-all-done.3 = bf16[8,288,896]{2,1,0:T(8,128)(2,1)} async-done(((bf16[8,288,896]{2,1,0:T(8,128)(2,1)}), bf16[8,288,896]{2,1,0:T(8,128)(2,1)}, u32[]{:S(2)}, u32[]{:S(2)}) %all-to-all-start.3) | async-done | bytes 4128800 | tf_op jit(solution)/shard_map/all_to_all | solution.py:127
  311.8 4.0 all-to-all-start
  315.8 4.8 copy.100
  320.6 5.7 fusion.19
  326.3 7.5 fusion
  333.8 5.7 convolution_convert_fusion.2
  339.5 7.4 fusion.5
  347.0 23.5 %copy.95 = bf16[1,288,7168]{1,0,2:T(2,128)(2,1)} copy(bf16[1,288,7168]{2,1,0:T(8,128)(2,1)} %fusion.5) | data formatting | bytes 8257536 | tf_op jit(solution)/shard_map/convert_element_type | solution.py:46
  370.5 0.5 broadcast.123
  371.0 118.8 %reduce.4 = bf16[7168,288]{1,0:T(8,128)(2,1)} reduce(bf16[7168,1,288]{2,1,0:T(2,128)(2,1)} %bitcast.97, bf16[]{:T(256)} %broadcast.123), dimensions={1}, to_apply=%bitcast.78.reduce_sub_computation | reduce | bytes 8257538
  489.8 10.8 %reshape.185 = bf16[8,2,129024]{2,1,0:T(2,128)(2,1)} reshape(bf16[7168,288]{1,0:T(8,128)(2,1)} %reduce.4) | data formatting | bytes 8257536
  500.6 5.9 all-to-all-start.4
  506.5 7.3 copy.91
  513.8 7.2 reshape_squeeze.4
  521.0 0.2 fusion.24
  521.3 143.3 %psum.37 = bf16[896,32]{0,1:T(8,128)(2,1)S(1)} all-reduce(bf16[896,32]{0,1:T(8,128)(2,1)S(1)} %fusion.24), channel_id=1, replica_groups=mesh['fsdp'=8,'ep'=32] {'ep'}, use_global_device_ids=true, to_apply=%region_12.13 | all-reduce | flops 28672 | bytes 114688 | tf_op jit(solution)/shard_map/psum | solution.py:116
  664.5 0.7 convert_element_type.188
  665.2 1.3 convolution_convert_fusion.1
  666.5 1.8 multiply_convert_fusion
  668.3 2.5 convert_element_type.181
  670.9 9.4 %convert_bitcast_fusion.1 = bf16[1,2048,896]{1,2,0:T(8,128)(2,1)} fusion(bf16[1152,896]{1,0:T(8,128)(2,1)S(1)} %convert_element_type.181, bf16[1152,2048]{1,0:T(8,128)(2,1)} %reshape_squeeze.4), kind=kOutput, calls=%fused_computation.21 | convolution fusion | flops 4229693440 | bytes 10452992 | tf_op jit(solution)/shard_map/dot_general | solution.py:103
  680.3 6.1 copy.98
  686.5 0.2 fusion.22
  686.8 0.1 reshape.158
  686.9 0.9 copy.97
  687.8 12.3 %reshape.186 = bf16[7168,1,288]{2,1,0:T(2,128)(2,1)} reshape(bf16[8,2,129024]{2,1,0:T(2,128)(2,1)} %all-to-all-done.4) | data formatting | bytes 8257536
  700.2 13.9 %convert_bitcast_fusion = f32[8,1,288,896]{2,1,3,0:T(1,128)} fusion(bf16[1,288,8,896]{1,0,3,2:T(2,128)(2,1)} %bitcast.98), kind=kLoop, calls=%fused_computation.1 | loop fusion | flops 2064384 | bytes 12386304 | tf_op jit(solution)/shard_map/convert_element_type | solution.py:50
  714.1 16.5 %copy.96 = f32[8,1,288,896]{3,0,2,1:T(8,128)} copy(f32[8,1,288,896]{2,1,3,0:T(1,128)} %convert_bitcast_fusion) | data formatting | bytes 16515072 | tf_op jit(solution)/shard_map/convert_element_type | solution.py:50
  730.6 10.3 %reshape.166 = f32[4,2,288,896]{3,1,0,2:T(2,128)} reshape(f32[8,1,288,896]{3,0,2,1:T(8,128)} %copy.96) | data formatting | bytes 16515072 | tf_op jit(solution)/shard_map/convert_element_type | solution.py:50
  740.9 14.0 %reduce_sum.82 = f32[4,288,896]{2,0,1:T(4,128)} reduce(f32[4,2,288,896]{3,1,0,2:T(2,128)} %reshape.166, f32[]{:T(128)} %constant.20.clone.1), dimensions={1}, to_apply=%region_16.17 | reduce | flops 1032192 | bytes 12386308 | tf_op jit(solution)/shard_map/reduce_sum | solution.py:51
  754.9 3.1 multiply_convert_fusion.1
  758.1 1.6 copy.99
  (40 shorter events, 1.1 us)
Async XLA Ops:
  8.0 2.9 copy-start
  20.8 78.7 %all-to-all-start.1 = ((bf16[32,36,896]{2,1,0:T(8,128)(2,1)}), bf16[32,36,896]{2,1,0:T(8,128)(2,1)S(1)}, u32[]{:S(2)}, u32[]{:S(2)}) async-start(bf16[32,36,896]{2,1,0:T(8,128)(2,1)} %select_select_fusion), calls=%async_computation.1 | async-start | bytes 4587520 | tf_op jit(solution)/shard_map/all_to_all | solution.py:80
  32.3 179.5 %all-reduce.3.cloned.1.call-start = ((), (), s32[]{:S(2)}) async-start(), calls=%async_computation.8 | async-start | bytes 4128768 | tf_op jit(solution)/shard_map/psum | solution.py:122
  33.0 181.0 %reduce-scatter.2.cloned.1.call-start = ((), (), s32[]{:S(2)}) async-start(), calls=%async_computation.6 | async-start | bytes 5308416 | tf_op jit(solution)/shard_map/reduce_scatter | solution.py:86
  110.4 0.9 copy-start.4
  110.4 1.0 copy-start.5
  110.4 1.3 copy-start.3
  110.4 396.1 %all-gather.2.cloned.1.call-start = ((), (), s32[]{:S(2)}) async-start(), calls=%async_computation.7 | async-start | bytes 5308416 | tf_op jit(solution)/shard_map/all_gather | solution.py:100
  236.7 15.5 %all-to-all-start.2 = ((f32[32,1,36]{2,1,0:T(1,128)}), f32[32,1,36]{2,1,0:T(1,128)S(1)}, u32[]{:S(2)}, u32[]{:S(2)}) async-start(f32[32,1,36]{2,1,0:T(1,128)} %get-tuple-element.42), calls=%async_computation.3 | async-start | bytes 32768 | tf_op jit(solution)/shard_map/all_to_all | solution.py:108
  256.1 8.4 %copy-start.6 = (f32[128,32]{0,1:T(8,128)S(1)}, f32[128,32]{0,1:T(8,128)}, u32[]{:S(2)}) copy-start(f32[128,32]{0,1:T(8,128)} %param.12) | copy-start | bytes 49156
  256.1 55.7 %all-to-all-start.3 = ((bf16[8,288,896]{2,1,0:T(8,128)(2,1)}), bf16[8,288,896]{2,1,0:T(8,128)(2,1)}, u32[]{:S(2)}, u32[]{:S(2)}) async-start(bf16[8,288,896]{2,1,0:T(8,128)(2,1)} %bitcast.99), calls=%async_computation.4 | async-start | bytes 8257536 | tf_op jit(solution)/shard_map/all_to_all | solution.py:127
  311.8 188.9 %all-to-all-start = ((bf16[32,1,36]{2,1,0:T(2,128)(2,1)}), bf16[32,1,36]{2,1,0:T(2,128)(2,1)S(1)}, u32[]{:S(2)}, u32[]{:S(2)}) async-start(bf16[32,1,36]{2,1,0:T(2,128)(2,1)} %copy.87), calls=%async_computation | async-start | bytes 32768 | tf_op jit(solution)/shard_map/all_to_all | solution.py:81
  500.6 187.2 %all-to-all-start.4 = ((bf16[8,2,129024]{2,1,0:T(2,128)(2,1)}), bf16[8,2,129024]{2,1,0:T(2,128)(2,1)}, u32[]{:S(2)}, u32[]{:S(2)}) async-start(bf16[8,2,129024]{2,1,0:T(2,128)(2,1)} %reshape.185), calls=%async_computation.5 | async-start | bytes 8257536 | tf_op jit(solution)/shard_map/all_to_all | solution.py:132
  680.3 6.3 copy-start.2
  740.9 18.7 %copy-start.1 = (bf16[128,896]{1,0:T(8,128)(2,1)S(1)}, bf16[128,896]{1,0:T(8,128)(2,1)}, u32[]{:S(2)}) copy-start(bf16[128,896]{1,0:T(8,128)(2,1)} %param.8) | copy-start | bytes 688132
Sparse Core Ops, SparseCore 0:
  36.6 175.1 all-reduce.2
Sparse Core Ops, SparseCore 1:
  110.5 34.9 reduce-scatter.1
  147.1 43.2 all-gather.1
where the time goes:
time: 778 us; the launch traced here: 768 us
  waiting for transfers between devices  216 us (28%)
  other arithmetic  166 us (21%)
  blocking collectives  164 us (21%)
  local copies, waits for them, and re-layouts  123 us (16%)
  matrix products  46.5 us (6%)
  starting transfers between devices  35.4 us (5%)
  between operations  16.2 us (2%)
    psum x1, blocking collectives, on_device(): lax.psum(router_part.astype(jnp.bfloat16), 'ep').astype(jnp.float32)  143 us
    unnamed x1, other arithmetic  119 us
    psum x1, waiting for transfers between devices, on_device(): lax.psum(partial_value.astype(jnp.float32).astype(jnp.bfloat16), 'ep')  96.3 us
    all_to_all x1, waiting for transfers between devices, on_device(): lax.all_to_all(packed, 'ep', split_axis=0, concat_axis=0, tiled=True)  66.4 us
    all_to_all x1, waiting for transfers between devices, on_device(): lax.all_to_all(jnp.repeat(initial, copies, axis=0), 'fsdp', split_axis=0,...  46.3 us
    unnamed x21, local copies, waits for them, and re-layouts  37.5 us
    convert_element_type x2, local copies, waits for them, and re-layouts, merge_copies(): returned.reshape(-1, copies, returned.shape[1], returned.shape[2])  26.8 us
    convert_element_type x1, local copies, waits for them, and re-layouts, orthogonalize(): return (factor * current.astype(jnp.float32)).astype(jnp.bfloat16)  23.5 us
  transfers between devices with their start and end apart: 8, of which 4 were waited for; matrix products, arithmetic and copies ran while one was open for 33% of the time, Pallas kernels for 0%

commit v1 on v0

v1 whole, which is shorter than its diff:
```python
import jax
import jax.numpy as jnp
from jax import lax
from jax.experimental import pallas as pl
from jax.experimental.pallas import tpu as pltpu
from jax.sharding import Mesh, PartitionSpec as P

D = 7168
LATENT = 288
ROUTE_SCALE = 2.827
NORM_EPS = 1e-07
COEF_A = 3.4445
COEF_B = -4.775
COEF_C = 2.0315
CAP = 36
SLOTS = 40
EXPERTS = 32
TOK = 128

FS = ("x", "c")
EP = ("z", "y")
f32 = jnp.float32
bf16 = jnp.bfloat16
VMEM_LIMIT = 48 * 1024 * 1024


def pack_kernel(routes_ref, tokens_ref, out_ref, pos_ref):
    expert_ids = lax.broadcasted_iota(jnp.int32, (EXPERTS, TOK), 0)
    chosen = jnp.zeros((EXPERTS, TOK), f32)
    for k in range(routes_ref.shape[0]):
        chosen = chosen + jnp.where(routes_ref[k : k + 1, :] == expert_ids, 1.0, 0.0)
    before = lax.broadcasted_iota(jnp.int32, (TOK, TOK), 0)
    after = lax.broadcasted_iota(jnp.int32, (TOK, TOK), 1)
    upper = jnp.where(before <= after, 1.0, 0.0).astype(bf16)
    counted = jnp.dot(chosen.astype(bf16), upper, preferred_element_type=f32)
    position = jnp.where(chosen > 0.0, counted - 1.0, -1.0)
    pos_ref[...] = position
    slot_ids = lax.broadcasted_iota(jnp.int32, (SLOTS, TOK), 0).astype(f32)
    tokens = tokens_ref[...]
    group = 8
    for start in range(0, EXPERTS, group):
        picks = [
            jnp.where(slot_ids == position[e : e + 1, :], 1.0, 0.0)
            for e in range(start, start + group)
        ]
        pick = jnp.concatenate(picks, axis=0).astype(bf16)
        rows = jnp.dot(pick, tokens, preferred_element_type=f32)
        for i in range(group):
            out_ref[start + i] = rows[i * SLOTS : (i + 1) * SLOTS].astype(bf16)


def pack(routes_t, tokens):
    width = tokens.shape[1]
    return pl.pallas_call(
        pack_kernel,
        out_shape=(
            jax.ShapeDtypeStruct((EXPERTS, SLOTS, width), bf16),
            jax.ShapeDtypeStruct((EXPERTS, TOK), f32),
        ),
        compiler_params=pltpu.CompilerParams(vmem_limit_bytes=VMEM_LIMIT),
        cost_estimate=pl.CostEstimate(flops=300_000_000, bytes_accessed=2_500_000, transcendentals=0),
    )(routes_t, tokens)


def upstream_kernel(rows_ref, down_ref, out_ref):
    out_ref[0] = lax.dot_general(
        rows_ref[...], down_ref[...], (((1,), (1,)), ((), ())), preferred_element_type=f32
    ).astype(bf16)


def upstream_partial(rows, down, parts):
    count, width = rows.shape
    share = down.shape[0] // parts
    return pl.pallas_call(
        upstream_kernel,
        grid=(parts,),
        in_specs=[
            pl.BlockSpec((count, width), lambda g: (0, 0)),
            pl.BlockSpec((share, width), lambda g: (g, 0)),
        ],
        out_specs=pl.BlockSpec((1, count, share), lambda g: (g, 0, 0)),
        out_shape=jax.ShapeDtypeStruct((parts, count, share), bf16),
        compiler_params=pltpu.CompilerParams(vmem_limit_bytes=VMEM_LIMIT),
        cost_estimate=pl.CostEstimate(
            flops=2 * count * width * down.shape[0], bytes_accessed=10_500_000, transcendentals=0
        ),
    )(rows, down)


def back_kernel(hidden_ref, down_ref, out_ref):
    part = jnp.dot(hidden_ref[0], down_ref[...], preferred_element_type=f32)

    @pl.when(pl.program_id(0) == 0)
    def _():
        out_ref[...] = part

    @pl.when(pl.program_id(0) > 0)
    def _():
        out_ref[...] += part


def hidden_times_down(hidden, down):
    parts, count, share = hidden.shape
    width = down.shape[1]
    return pl.pallas_call(
        back_kernel,
        grid=(parts,),
        in_specs=[
            pl.BlockSpec((1, count, share), lambda g: (g, 0, 0)),
            pl.BlockSpec((share, width), lambda g: (g, 0)),
        ],
        out_specs=pl.BlockSpec((count, width), lambda g: (0, 0)),
        out_shape=jax.ShapeDtypeStruct((count, width), f32),
        compiler_params=pltpu.CompilerParams(vmem_limit_bytes=VMEM_LIMIT),
        cost_estimate=pl.CostEstimate(
            flops=2 * count * width * down.shape[0], bytes_accessed=12_500_000, transcendentals=0
        ),
    )(hidden, down)


def grad_down_kernel(hidden_ref, rows_ref, gate_ref, out_ref, scaled_ref):
    @pl.when(pl.program_id(0) == 0)
    def _():
        scaled_ref[...] = (gate_ref[...] * rows_ref[...].astype(f32)).astype(bf16)

    out_ref[0] = lax.dot_general(
        hidden_ref[0], scaled_ref[...], (((0,), (0,)), ((), ())), preferred_element_type=f32
    ).astype(bf16)


def grad_down_of(hidden, rows, gate):
    parts, count, share = hidden.shape
    width = rows.shape[1]
    return pl.pallas_call(
        grad_down_kernel,
        grid=(parts,),
        in_specs=[
            pl.BlockSpec((1, count, share), lambda g: (g, 0, 0)),
            pl.BlockSpec((count, width), lambda g: (0, 0)),
            pl.BlockSpec((count, 1), lambda g: (0, 0)),
        ],
        out_specs=pl.BlockSpec((1, share, width), lambda g: (0, g, 0)),
        out_shape=jax.ShapeDtypeStruct((1, parts * share, width), bf16),
        scratch_shapes=[pltpu.VMEM((count, width), bf16)],
        compiler_params=pltpu.CompilerParams(vmem_limit_bytes=VMEM_LIMIT),
        cost_estimate=pl.CostEstimate(
            flops=2 * count * width * parts * share, bytes_accessed=12_500_000, transcendentals=0
        ),
    )(hidden, rows, gate)


def exchange(value, axes):
    return lax.all_to_all(value, axes, split_axis=0, concat_axis=0, tiled=True)


def spread(value, axes, copies):
    return exchange(jnp.broadcast_to(value[None], (copies,) + value.shape), axes)


def muon(attention):
    mats, latent, width = attention.shape
    got = exchange(attention, "y")
    part = jnp.sum(got.astype(f32), axis=0).astype(bf16)
    got = exchange(part.reshape(8, latent // 8, width), "z")
    part = jnp.sum(got.astype(f32), axis=0).astype(bf16)
    summed = lax.all_gather(part, "z", axis=0, tiled=False).reshape(latent, width)
    gram = lax.dot_general(summed, summed, (((1,), (1,)), ((), ())), preferred_element_type=f32)
    got = exchange(gram.reshape(8, latent // 8, latent), FS)
    gram = spread(jnp.sum(got, axis=0), FS, 8).reshape(latent, latent)
    eye = jnp.eye(latent, dtype=f32)
    norm = jnp.sqrt(jnp.sum(gram * eye)) + NORM_EPS
    inverse = 1.0 / norm
    dot = lambda a, b: jnp.dot(a, b, precision=lax.Precision.HIGHEST)
    first = gram * inverse * inverse
    poly_first = COEF_A * eye + COEF_B * first + COEF_C * dot(first, first)
    second = dot(poly_first, dot(first, poly_first))
    poly_second = COEF_A * eye + COEF_B * second + COEF_C * dot(second, second)
    factor = 0.2 * jnp.sqrt(f32(max(LATENT, D)))
    both = dot(poly_second, poly_first) * (factor * inverse)
    high = both.astype(bf16)
    low = (both - high.astype(f32)).astype(bf16)
    mine = jnp.dot(high, summed, preferred_element_type=f32) + jnp.dot(
        low, summed, preferred_element_type=f32
    )
    return lax.all_gather(mine.astype(bf16), "y", axis=0, tiled=False)


def on_device(
    out_grad,
    router_input,
    router_weight,
    routes,
    balance_grad,
    saved_hidden,
    expert_down,
    attention_grads,
):
    width = out_grad.shape[1]
    down = expert_down[0]
    share = saved_hidden.shape[3]
    count = CAP * EXPERTS
    hidden_share = jnp.swapaxes(saved_hidden[0], 0, 1).reshape(count, share)
    hidden = lax.all_gather(hidden_share, FS, axis=0, tiled=False)

    weight_t = router_weight.T
    input_f = router_input.astype(f32)
    partial_logits = lax.dot_general(
        weight_t, input_f, (((1,), (1,)), ((), ())), precision=lax.Precision.HIGHEST
    )
    packed, position = pack(routes.T, out_grad)
    rows_got = exchange(packed, EP)
    logits = jnp.sum(spread(partial_logits, FS, 8), axis=0)
    muon_update = muon(attention_grads[0])

    scores = jax.nn.sigmoid(logits)
    chosen = position >= 0.0
    selected = chosen.astype(f32)
    score_total = jnp.sum(selected * scores, axis=0, keepdims=True)
    gates = (selected * ROUTE_SCALE * scores / score_total).astype(bf16).astype(f32)
    slot_ids = jnp.arange(SLOTS, dtype=jnp.int32).astype(f32)
    matches = position[:, None, :] == slot_ids[None, :, None]
    slot_gates = jnp.sum(jnp.where(matches, gates[:, None, :], 0.0), axis=2)
    gate_got = exchange(slot_gates, EP)
    gate_column = gate_got[:, :CAP].T.reshape(count, 1)

    rows = jnp.swapaxes(rows_got[:, :CAP], 0, 1).reshape(count, width)
    back = hidden_times_down(hidden, down)
    gate_part = jnp.sum(back * rows.astype(f32), axis=1).reshape(CAP, EXPERTS).T
    returned = exchange(jnp.pad(gate_part, ((0, 0), (0, SLOTS - CAP))), EP)
    back_part = jnp.sum(jnp.where(matches, returned[:, :, None], 0.0), axis=1)
    gate_back = jnp.sum(spread(back_part, FS, 8), axis=0)

    upstream = lax.psum_scatter(
        upstream_partial(rows, down, 8), FS, scatter_dimension=0, tiled=True
    )
    grad_hidden = (gate_column * upstream.reshape(count, share).astype(f32)).astype(bf16)
    grad_hidden = jnp.swapaxes(grad_hidden.reshape(CAP, EXPERTS, share), 0, 1)[None]
    grad_down = grad_down_of(hidden, rows, gate_column)

    weighted = jnp.sum(selected * gate_back * scores, axis=0, keepdims=True) / score_total
    score_grad = balance_grad.T + selected * (ROUTE_SCALE / score_total) * (gate_back - weighted)
    logit_grad = score_grad * scores * (1.0 - scores)
    router_part = jnp.dot(logit_grad, input_f, precision=lax.Precision.HIGHEST)
    router_got = exchange(router_part, EP)
    router_row = jnp.sum(router_got.reshape(EXPERTS, width), axis=0)
    router_grad = spread(router_row.reshape(1, width), EP, EXPERTS).reshape(EXPERTS, width).T
    token_grad = lax.dot_general(
        logit_grad, weight_t, (((0,), (0,)), ((), ())), precision=lax.Precision.HIGHEST
    ).astype(bf16)
    return (grad_hidden, grad_down, router_grad, token_grad, muon_update)


def solution(mesh):
    split = Mesh(mesh.devices.reshape(4, 2, 8, 4), ("x", "c", "z", "y"))
    in_specs = (
        P(EP, FS),
        P(EP, FS),
        P(FS, None),
        P(EP, None),
        P(EP, None),
        P(EP, None, None, FS),
        P(EP, None, FS),
        P(EP, None, None, FS),
    )
    out_specs = (
        P(EP, None, None, FS),
        P(EP, None, FS),
        P(FS, None),
        P(EP, FS),
        P(None, None, FS),
    )
    return jax.shard_map(
        on_device, mesh=split, in_specs=in_specs, out_specs=out_specs, check_vma=False
    )
```

time: 778 us -> 303 us (0.39); the launches traced: 768 us -> 300 us
  other arithmetic: 166 us -> 7.79 us
  waiting for transfers between devices: 216 us -> 89.3 us
  local copies, waits for them, and re-layouts: 123 us -> 15.9 us
  blocking collectives: 164 us -> 94.9 us
  matrix products: 46.5 us -> 8.95 us
  Pallas kernels: 0 us -> 32.6 us
    psum x2 -> x0, blocking collectives: 164 us -> none  [the longest x1 143 us: on_device(): lax.psum(router_part.astype(jnp.bfloat16), 'ep').astype(jnp.float32)]
    unnamed x1 -> x0, other arithmetic: 119 us -> none
    psum x1 -> x0, waiting for transfers between devices: 96.3 us -> none  [on_device(): lax.psum(partial_value.astype(jnp.float32).astype(jnp.bfloat16), 'ep')]
    all_to_all x0 -> x3, blocking collectives: none -> 69.3 us  [exchange(): return lax.all_to_all(value, axes, split_axis=0, concat_axis=0, tiled=True)]
    convert_element_type x9 -> x0, local copies, waits for them, and re-layouts: 57.4 us -> none  [the longest x2 26.8 us: merge_copies(): returned.reshape(-1, copies, returned.shape[1], returned.shape[2])]
    dot_general x9 -> x11, matrix products: 46.5 us -> 8.95 us  [the longest x5 4.96 us: muon(): dot = lambda a, b: jnp.dot(a, b, precision=lax.Precision.HIGHEST)]
    pallas_call x0 -> x4, Pallas kernels: none -> 32.6 us  [the longest x1 12.4 us: hidden_times_down(): pl.pallas_call(back_kernel, grid=(parts,), in_specs=[pl.BlockSpec((1, cou...]
    all_to_all x5 -> x8, waiting for transfers between devices: 119 us -> 88.6 us  [exchange(): return lax.all_to_all(value, axes, split_axis=0, concat_axis=0, tiled=True)]
  transfers between devices with their start and end apart: 8 -> 11, of which waited for: 4 -> 7; matrix products, arithmetic and copies ran while one was open for 33% -> 8% of each run, Pallas kernels for 0% -> 11%
where the time goes in v1:
time: 303 us; the launch traced here: 300 us
  blocking collectives  94.9 us (31%)
  waiting for transfers between devices  89.3 us (29%)
  starting transfers between devices  36.2 us (12%)
  Pallas kernels  32.6 us (11%)
  local copies, waits for them, and re-layouts  15.9 us (5%)
  between operations  14.8 us (5%)
  matrix products  8.95 us (3%)
  other arithmetic  7.79 us (3%)
    all_to_all x8, waiting for transfers between devices, exchange(): return lax.all_to_all(value, axes, split_axis=0, concat_axis=0, tiled=True)  88.6 us
    all_to_all x3, blocking collectives, exchange(): return lax.all_to_all(value, axes, split_axis=0, concat_axis=0, tiled=True)  69.3 us
    all_to_all x8, starting transfers between devices, exchange(): return lax.all_to_all(value, axes, split_axis=0, concat_axis=0, tiled=True)  35.9 us
    all_gather x1, blocking collectives, muon(): lax.all_gather(part, 'z', axis=0, tiled=False).reshape(latent, width)  25.6 us
    pallas_call x1, Pallas kernels, hidden_times_down(): pl.pallas_call(back_kernel, grid=(parts,), in_specs=[pl.BlockSpec((1, cou...  12.4 us
    pallas_call x1, Pallas kernels, grad_down_of(): pl.pallas_call(grad_down_kernel, grid=(parts,), in_specs=[pl.BlockSpec((1...  10.5 us
    unnamed x18, local copies, waits for them, and re-layouts  8.6 us
    pallas_call x1, Pallas kernels, upstream_partial(): pl.pallas_call(upstream_kernel, grid=(parts,), in_specs=[pl.BlockSpec((co...  7.45 us
  transfers between devices with their start and end apart: 11, of which 7 were waited for; matrix products, arithmetic and copies ran while one was open for 8% of the time, Pallas kernels for 11%

profile of v1, /device:TPU:2, one launch (start us, length us, event | category | flops | bytes accessed | tf_op | source)
XLA Modules:
  0.0 300.4 jit_solution(653358661192381403)
XLA Ops:
  7.2 0.7 all-gather.6.cloned.1.call-update
  7.9 30.5 %all_to_all.70 = bf16[4,288,896]{2,1,0:T(8,128)(2,1)S(1)} all-to-all(bf16[4,288,896]{2,1,0:T(8,128)(2,1)} %bitcast.68), channel_id=1, replica_groups=mesh['x'=4,'c'=2,'z'=8,'y'=4] {'y'}, dimensions={0} | all-to-all | bytes 4128768 | tf_op jit(solution)/shard_map/all_to_all | solution.py:153
  38.4 0.6 reduce_sum.122
  39.0 0.1 reshape.94
  39.1 25.6 %all_to_all.71 = bf16[8,36,896]{2,1,0:T(8,128)(2,1)S(1)} all-to-all(bf16[8,36,896]{2,1,0:T(8,128)(2,1)S(1)} %reshape.94), channel_id=1, replica_groups=mesh['x'=4,'c'=2,'z'=8,'y'=4] {'z'}, dimensions={0} | all-to-all | bytes 1032192 | tf_op jit(solution)/shard_map/all_to_all | solution.py:153
  64.7 0.1 reduce_sum.123
  64.8 25.6 %all-gather.2 = bf16[8,36,896]{2,1,0:T(8,128)(2,1)S(1)} all-gather(bf16[1,36,896]{2,1,0:T(8,128)(2,1)S(1)} %bitcast.72), channel_id=2, replica_groups=mesh['x'=4,'c'=2,'z'=8,'y'=4] {'z'}, dimensions={0}, use_global_device_ids=true | all-gather | bytes 580608 | tf_op jit(solution)/shard_map/all_gather | solution.py:166
  90.4 0.1 reshape.103
  90.5 0.5 fusion.14
  91.1 13.2 %all_to_all.72 = f32[8,36,288]{2,1,0:T(8,128)S(1)} all-to-all(f32[8,36,288]{2,1,0:T(8,128)S(1)} %fusion.14), channel_id=1, replica_groups=mesh['x'=4,'c'=2,'z'=8,'y'=4] {'x','c'}, dimensions={0} | all-to-all | bytes 663552 | tf_op jit(solution)/shard_map/all_to_all | solution.py:153
  104.3 0.8 broadcast_in_dim.64
  105.1 4.9 %all-to-all-start.10 = ((f32[8,36,288]{2,1,0:T(8,128)}), f32[8,36,288]{2,1,0:T(8,128)S(1)}, u32[]{:S(2)}, u32[]{:S(2)}) async-start(f32[8,36,288]{2,1,0:T(8,128)} %broadcast_in_dim.64), calls=%async_computation.11 | async-start | bytes 983040 | tf_op jit(solution)/shard_map/all_to_all | solution.py:153
  110.0 2.3 shard_map.119
  112.3 0.1 reshape.101
  112.4 6.2 %all-to-all-done.10 = f32[8,36,288]{2,1,0:T(8,128)S(1)} async-done(((f32[8,36,288]{2,1,0:T(8,128)}), f32[8,36,288]{2,1,0:T(8,128)S(1)}, u32[]{:S(2)}, u32[]{:S(2)}) %all-to-all-start.10) | async-done | bytes 331808 | tf_op jit(solution)/shard_map/all_to_all | solution.py:153
  118.6 4.8 %all-to-all-start.2 = ((bf16[32,40,896]{2,1,0:T(8,128)(2,1)}), bf16[32,40,896]{2,1,0:T(8,128)(2,1)}, u32[]{:S(2)}, u32[]{:S(2)}) async-start(bf16[32,40,896]{2,1,0:T(8,128)(2,1)} %get-tuple-element.8), calls=%async_computation.2 | async-start | bytes 4587520 | tf_op jit(solution)/shard_map/all_to_all | solution.py:153
  123.4 0.0 all-gather.8.cloned.1.call-start
  123.4 0.8 select_reduce_fusion
  125.1 1.0 fusion.2
  126.1 1.0 fusion.15
  127.1 1.0 fusion.16
  128.1 1.0 fusion.1
  129.1 1.0 convolution_multiply_fusion
  130.1 0.4 fusion.8
  130.5 1.2 fusion
  131.8 0.2 reduce-scatter.2.cloned.1.call-start
  132.0 46.5 %all-to-all-done.2 = bf16[32,40,896]{2,1,0:T(8,128)(2,1)} async-done(((bf16[32,40,896]{2,1,0:T(8,128)(2,1)}), bf16[32,40,896]{2,1,0:T(8,128)(2,1)}, u32[]{:S(2)}, u32[]{:S(2)}) %all-to-all-start.2) | async-done | bytes 2293792 | tf_op jit(solution)/shard_map/all_to_all | solution.py:153
  178.5 1.8 slice_bitcast_fusion
  180.3 0.3 copy.25
  180.6 1.8 copy-done.1
  182.4 7.4 %shard_map.120 = bf16[8,1152,256]{2,1,0:T(8,128)(2,1)} custom-call(bf16[1152,896]{1,0:T(8,128)(2,1)S(1)} %bitcast.63, bf16[2048,896]{1,0:T(8,128)(2,1)S(1)} %bitcast.65), custom_call_target="tpu_custom_call" | custom-call | flops 4227858432 | bytes 10500000 | tf_op jit(solution)/shard_map/pallas_call | solution.py:74
  189.9 0.9 copy-done.5
  190.7 0.3 fusion.13
  191.1 2.0 copy-done.2
  193.1 12.4 %shard_map.122 = f32[1152,896]{1,0:T(8,128)} custom-call(bf16[8,1152,256]{2,1,0:T(8,128)(2,1)} %all-gather.6.cloned.1.call-done.hidden_ref, bf16[2048,896]{1,0:T(8,128)(2,1)S(1)} %bitcast.66), custom_call_target="tpu_custom_call" | custom-call | flops 4227858432 | bytes 12500000 | tf_op jit(solution)/shard_map/pallas_call | solution.py:105
  205.5 2.7 multiply_reduce_fusion
  208.3 0.1 reshape.92
  208.4 0.7 copy.28
  209.0 5.2 %all-to-all-start.3 = ((f32[32,1,40]{2,1,0:T(1,128)}), f32[32,1,40]{2,1,0:T(1,128)S(1)}, u32[]{:S(2)}, u32[]{:S(2)}) async-start(f32[32,1,40]{2,1,0:T(1,128)} %copy.28), calls=%async_computation.4 | async-start | bytes 32768 | tf_op jit(solution)/shard_map/all_to_all | solution.py:153
  214.3 9.6 %all-to-all-done.3 = f32[32,1,40]{2,1,0:T(1,128)S(1)} async-done(((f32[32,1,40]{2,1,0:T(1,128)}), f32[32,1,40]{2,1,0:T(1,128)S(1)}, u32[]{:S(2)}, u32[]{:S(2)}) %all-to-all-start.3) | async-done | bytes 5152 | tf_op jit(solution)/shard_map/all_to_all | solution.py:153
  223.9 0.7 broadcast_in_dim.34
  224.6 4.7 %all-to-all-start = ((f32[8,32,128]{2,1,0:T(8,128)}), f32[8,32,128]{2,1,0:T(8,128)S(1)}, u32[]{:S(2)}, u32[]{:S(2)}) async-start(f32[8,32,128]{2,1,0:T(8,128)} %broadcast_in_dim.34), calls=%async_computation | async-start | bytes 262144 | tf_op jit(solution)/shard_map/all_to_all | solution.py:153
  229.3 0.3 fusion.5
  229.6 4.4 %all-to-all-done = f32[8,32,128]{2,1,0:T(8,128)S(1)} async-done(((f32[8,32,128]{2,1,0:T(8,128)}), f32[8,32,128]{2,1,0:T(8,128)S(1)}, u32[]{:S(2)}, u32[]{:S(2)}) %all-to-all-start) | async-done | bytes 131104 | tf_op jit(solution)/shard_map/all_to_all | solution.py:153
  234.0 0.7 broadcast_in_dim.62
  234.7 4.7 %all-to-all-start.4 = ((f32[8,32,128]{2,1,0:T(8,128)}), f32[8,32,128]{2,1,0:T(8,128)S(1)}, u32[]{:S(2)}, u32[]{:S(2)}) async-start(f32[8,32,128]{2,1,0:T(8,128)} %broadcast_in_dim.62), calls=%async_computation.5 | async-start | bytes 262144 | tf_op jit(solution)/shard_map/all_to_all | solution.py:153
  239.4 4.7 %all-to-all-done.4 = f32[8,32,128]{2,1,0:T(8,128)S(1)} async-done(((f32[8,32,128]{2,1,0:T(8,128)}), f32[8,32,128]{2,1,0:T(8,128)S(1)}, u32[]{:S(2)}, u32[]{:S(2)}) %all-to-all-start.4) | async-done | bytes 131104 | tf_op jit(solution)/shard_map/all_to_all | solution.py:153
  244.2 0.9 fusion.4
  245.1 3.8 %all-to-all-start.1 = ((f32[32,1,40]{2,1,0:T(1,128)}), f32[32,1,40]{2,1,0:T(1,128)S(1)}, u32[]{:S(2)}, u32[]{:S(2)}) async-start(f32[32,1,40]{2,1,0:T(1,128)} %bitcast.2), calls=%async_computation.1 | async-start | bytes 32768 | tf_op jit(solution)/shard_map/all_to_all | solution.py:153
  249.0 1.3 convolution_convert_fusion
  250.2 0.2 convolution_bitcast_fusion
  250.5 0.8 copy.29
  251.2 7.4 %all-to-all-done.1 = f32[32,1,40]{2,1,0:T(1,128)S(1)} async-done(((f32[32,1,40]{2,1,0:T(1,128)}), f32[32,1,40]{2,1,0:T(1,128)S(1)}, u32[]{:S(2)}, u32[]{:S(2)}) %all-to-all-start.1) | async-done | bytes 5152 | tf_op jit(solution)/shard_map/all_to_all | solution.py:153
  258.6 3.9 %all-to-all-start.5 = ((f32[32,1,896]{2,1,0:T(1,128)}), f32[32,1,896]{2,1,0:T(1,128)S(1)}, u32[]{:S(2)}, u32[]{:S(2)}) async-start(f32[32,1,896]{2,1,0:T(1,128)} %copy.29), calls=%async_computation.6 | async-start | bytes 229376 | tf_op jit(solution)/shard_map/all_to_all | solution.py:153
  262.5 0.1 copy.24
  262.6 0.6 reshape.104.gate_ref
  263.2 9.7 %all-to-all-done.5 = f32[32,1,896]{2,1,0:T(1,128)S(1)} async-done(((f32[32,1,896]{2,1,0:T(1,128)}), f32[32,1,896]{2,1,0:T(1,128)S(1)}, u32[]{:S(2)}, u32[]{:S(2)}) %all-to-all-start.5) | async-done | bytes 114720 | tf_op jit(solution)/shard_map/all_to_all | solution.py:153
  272.9 0.1 reduce_sum.121
  273.0 0.7 broadcast_in_dim.63
  273.7 3.9 %all-to-all-start.6 = ((f32[32,1,896]{2,1,0:T(1,128)}), f32[32,1,896]{2,1,0:T(1,128)S(1)}, u32[]{:S(2)}, u32[]{:S(2)}) async-start(f32[32,1,896]{2,1,0:T(1,128)} %broadcast_in_dim.63), calls=%async_computation.7 | async-start | bytes 229376 | tf_op jit(solution)/shard_map/all_to_all | solution.py:153
  277.6 10.5 %shard_map.121 = bf16[1,2048,896]{2,1,0:T(8,128)(2,1)} custom-call(bf16[8,1152,256]{2,1,0:T(8,128)(2,1)} %all-gather.6.cloned.1.call-done.hidden_ref, bf16[1152,896]{1,0:T(8,128)(2,1)S(1)} %bitcast.64, f32[1152,1]{1,0:T(8,128)S(1)} %reshape.104.gate_ref), custom_call_target="tpu_custom_call" | custom-call | flops 4227858432 | bytes 12500000 | tf_op jit(solution)/shard_map/pallas_call | solution.py:134
  288.1 0.7 copy.32
  288.7 2.1 fusion.6
  290.8 3.0 %copy.34 = bf16[4,288,896]{2,1,0:T(8,128)(2,1)} copy(bf16[4,288,896]{2,1,0:T(8,128)(2,1)} %bitcast.69) | data formatting | bytes 4128768
  (30 shorter events, 0.4 us)
Async XLA Ops:
  7.2 182.7 %copy-start = (bf16[128,896]{1,0:T(8,128)(2,1)S(1)}, bf16[128,896]{1,0:T(8,128)(2,1)}, u32[]{:S(2)}) copy-start(bf16[128,896]{1,0:T(8,128)(2,1)} %param.9) | copy-start | bytes 688132
  7.2 183.9 %all-gather.6.cloned.1.call-start = ((), (), s32[]{:S(2)}) async-start(), calls=%async_computation.13 | async-start | bytes 5308416 | tf_op jit(solution)/shard_map/all_gather | solution.py:203
  90.5 19.5 %copy-start.3 = (bf16[128,896]{1,0:T(8,128)(2,1)S(1)}, bf16[128,896]{1,0:T(8,128)(2,1)}, u32[]{:S(2)}) copy-start(bf16[128,896]{1,0:T(8,128)(2,1)} %tokens_ref.1) | copy-start | bytes 688132
  90.5 19.5 %copy-start.4 = (s32[128,8]{0,1:T(8,128)S(1)}, s32[128,8]{0,1:T(8,128)}, u32[]{:S(2)}) copy-start(s32[128,8]{0,1:T(8,128)} %param.11) | copy-start | bytes 12292
  105.1 13.4 %all-to-all-start.10 = ((f32[8,36,288]{2,1,0:T(8,128)}), f32[8,36,288]{2,1,0:T(8,128)S(1)}, u32[]{:S(2)}, u32[]{:S(2)}) async-start(f32[8,36,288]{2,1,0:T(8,128)} %broadcast_in_dim.64), calls=%async_computation.11 | async-start | bytes 983040 | tf_op jit(solution)/shard_map/all_to_all | solution.py:153
  118.6 59.9 %all-to-all-start.2 = ((bf16[32,40,896]{2,1,0:T(8,128)(2,1)}), bf16[32,40,896]{2,1,0:T(8,128)(2,1)}, u32[]{:S(2)}, u32[]{:S(2)}) async-start(bf16[32,40,896]{2,1,0:T(8,128)(2,1)} %get-tuple-element.8), calls=%async_computation.2 | async-start | bytes 4587520 | tf_op jit(solution)/shard_map/all_to_all | solution.py:153
  123.4 116.1 %all-gather.8.cloned.1.call-start = ((), (), s32[]{:S(2)}) async-start(), calls=%async_computation.14 | async-start | bytes 2580480 | tf_op jit(solution)/shard_map/all_gather | solution.py:185
  131.8 157.0 %reduce-scatter.2.cloned.1.call-start = ((), (), s32[]{:S(2)}) async-start(), calls=%async_computation.12 | async-start | bytes 5308416 | tf_op jit(solution)/shard_map/reduce_scatter | solution.py:233
  180.3 2.0 copy-start.1
  189.8 0.9 copy-start.5
  191.1 2.0 copy-start.2
  205.5 38.7 %copy-start.6 = (f32[128,32]{0,1:T(8,128)S(1)}, f32[128,32]{0,1:T(8,128)}, u32[]{:S(2)}) copy-start(f32[128,32]{0,1:T(8,128)} %param.12) | copy-start | bytes 49156
  209.0 14.9 %all-to-all-start.3 = ((f32[32,1,40]{2,1,0:T(1,128)}), f32[32,1,40]{2,1,0:T(1,128)S(1)}, u32[]{:S(2)}, u32[]{:S(2)}) async-start(f32[32,1,40]{2,1,0:T(1,128)} %copy.28), calls=%async_computation.4 | async-start | bytes 32768 | tf_op jit(solution)/shard_map/all_to_all | solution.py:153
  224.6 9.4 %all-to-all-start = ((f32[8,32,128]{2,1,0:T(8,128)}), f32[8,32,128]{2,1,0:T(8,128)S(1)}, u32[]{:S(2)}, u32[]{:S(2)}) async-start(f32[8,32,128]{2,1,0:T(8,128)} %broadcast_in_dim.34), calls=%async_computation | async-start | bytes 262144 | tf_op jit(solution)/shard_map/all_to_all | solution.py:153
  234.7 9.4 %all-to-all-start.4 = ((f32[8,32,128]{2,1,0:T(8,128)}), f32[8,32,128]{2,1,0:T(8,128)S(1)}, u32[]{:S(2)}, u32[]{:S(2)}) async-start(f32[8,32,128]{2,1,0:T(8,128)} %broadcast_in_dim.62), calls=%async_computation.5 | async-start | bytes 262144 | tf_op jit(solution)/shard_map/all_to_all | solution.py:153
  245.1 13.5 %all-to-all-start.1 = ((f32[32,1,40]{2,1,0:T(1,128)}), f32[32,1,40]{2,1,0:T(1,128)S(1)}, u32[]{:S(2)}, u32[]{:S(2)}) async-start(f32[32,1,40]{2,1,0:T(1,128)} %bitcast.2), calls=%async_computation.1 | async-start | bytes 32768 | tf_op jit(solution)/shard_map/all_to_all | solution.py:153
  258.6 14.3 %all-to-all-start.5 = ((f32[32,1,896]{2,1,0:T(1,128)}), f32[32,1,896]{2,1,0:T(1,128)S(1)}, u32[]{:S(2)}, u32[]{:S(2)}) async-start(f32[32,1,896]{2,1,0:T(1,128)} %copy.29), calls=%async_computation.6 | async-start | bytes 229376 | tf_op jit(solution)/shard_map/all_to_all | solution.py:153
  273.7 14.3 %all-to-all-start.6 = ((f32[32,1,896]{2,1,0:T(1,128)}), f32[32,1,896]{2,1,0:T(1,128)S(1)}, u32[]{:S(2)}, u32[]{:S(2)}) async-start(f32[32,1,896]{2,1,0:T(1,128)} %broadcast_in_dim.63), calls=%async_computation.7 | async-start | bytes 229376 | tf_op jit(solution)/shard_map/all_to_all | solution.py:153
Sparse Core Ops, SparseCore 0:
  9.8 38.8 all-gather.5
  131.9 45.1 all-gather.7
  190.0 33.7 reduce-scatter.1
